TPU v7x, 32 devices: a whole 2x2x4 slice. The times are simulated.
32 devices in a mesh: pair: 2 (over x), grow: 4 (over y, core), gcol: 4 (over z).
Axes of the slice: x: 2, y: 2, z: 4, core: 2. Of those that a mesh axis runs over, the one named last changes fastest.
Arguments:
- pair_elements: bfloat16 [1792, 8192], P('pair', ('grow', 'gcol')), may hold values from -0.75 to 0.75
- coulomb_root: float32 [8192], replicated, may hold values from 0.25 to 1
Outputs:
- factored: float32 [8192, 8192], P('grow', ('gcol', 'pair'))
All inputs are finite; a program needn't handle non-finite values.
Results may differ from a plain program's by a relative error of at most 0.0003.
Values may be sent and summed in bfloat16 or wider, within the bound.
A program may use at most 128 MiB of HBM per device.

v0:
```python
import jax
import jax.numpy as jnp
from jax import lax
from jax.sharding import PartitionSpec as P

PANEL = 512
PANELS = 2


def from_root(array, axis, root):
    mine = lax.axis_index(axis) == root
    return lax.psum(jnp.where(mine, array, jnp.zeros_like(array)), axis)


def body(pair_elements, coulomb_root):
    grid_total = coulomb_root.shape[0]
    tile_rows = grid_total // lax.axis_size("grow")
    tile_cols = grid_total // (lax.axis_size("gcol") * lax.axis_size("pair"))
    row_index = lax.axis_index("grow")
    col_index = lax.axis_index("gcol")
    gathered = lax.all_gather(pair_elements, ("grow", "gcol"), axis=1, tiled=True)
    row_block = lax.dynamic_slice_in_dim(gathered, row_index * tile_rows, tile_rows, 1)
    col_block = lax.dynamic_slice_in_dim(gathered, col_index * tile_rows, tile_rows, 1)
    flipped = lax.psum_scatter(
        lax.dot_general(
            col_block, row_block, (((0,), (0,)), ((), ())), preferred_element_type=jnp.float32
        ),
        "pair",
        scatter_dimension=0,
        tiled=True,
    )
    chi_tile = flipped.T
    row_base = row_index * tile_rows
    col_base = lax.axis_index(("gcol", "pair")) * tile_cols
    row_ids = row_base + jnp.arange(tile_rows, dtype=jnp.int32)[:, None]
    col_ids = col_base + jnp.arange(tile_cols, dtype=jnp.int32)[None, :]
    scale_rows = lax.dynamic_slice_in_dim(coulomb_root, row_base, tile_rows, 0)
    scale_cols = lax.dynamic_slice_in_dim(coulomb_root, col_base, tile_cols, 0)
    working = (
        jnp.where(row_ids == col_ids, 1.0, 0.0).astype(jnp.float32)
        + scale_rows[:, None] * chi_tile * scale_cols[None, :]
    )
    packed = jnp.zeros((tile_rows, tile_cols), jnp.float32)
    covered = jnp.zeros((tile_rows, tile_cols), bool)
    owner_width = min(PANEL, tile_cols)
    for step_index in range(PANELS):
        first = step_index * PANEL
        gathered_cols = []
        for owner in range(max(1, PANEL // tile_cols)):
            global_col = first + owner * owner_width
            local_col = global_col % tile_cols
            gathered_cols.append(
                from_root(
                    working[:, local_col : local_col + owner_width],
                    ("gcol", "pair"),
                    global_col // tile_cols,
                )
            )
        panel_cols = jnp.concatenate(gathered_cols, axis=1)
        local_row = first % tile_rows
        diag_block, panel_rows = (
            from_root(panel_cols[local_row : local_row + PANEL], "grow", first // tile_rows),
            from_root(working[local_row : local_row + PANEL], "grow", first // tile_rows),
        )
        factor = jnp.linalg.cholesky(diag_block)
        low_rows = lax.linalg.triangular_solve(
            factor, panel_cols, left_side=False, lower=True, transpose_a=True
        )
        low_cols = lax.linalg.triangular_solve(factor, panel_rows, left_side=True, lower=True)
        working = working - jnp.dot(low_rows, low_cols, precision=lax.Precision.HIGHEST)
        col_pos = col_ids - first
        in_cols = (col_pos >= 0) & (col_pos < PANEL) & (row_ids >= col_ids)
        col_vals = jnp.take(low_rows, jnp.clip(col_pos[0], 0, PANEL - 1), axis=1)
        row_pos = row_ids - first
        in_rows = (row_pos >= 0) & (row_pos < PANEL) & (col_ids > row_ids)
        row_vals = jnp.take(low_cols, jnp.clip(row_pos[:, 0], 0, PANEL - 1), axis=0)
        packed = packed + jnp.where(in_cols, col_vals, 0.0) + jnp.where(in_rows, row_vals, 0.0)
        covered = covered | in_cols | in_rows
    return jnp.where(covered, packed, working)


def solution(mesh):
    return jax.shard_map(
        body,
        mesh=mesh,
        in_specs=(P("pair", ("grow", "gcol")), P()),
        out_specs=P("grow", ("gcol", "pair")),
        check_vma=False,
    )
```

profile of v0, /device:TPU:0, one launch (start us, length us, event | category | flops | bytes accessed | tf_op | source)
XLA Modules:
  0.0 1215.4 jit_solution(15277184497236068876)
XLA Ops:
  7.3 122.0 %all-gather.2.cloned.1.call-done = bf16[896,8192]{1,0:T(8,128)(2,1)} async-done(((bf16[896,512]{1,0:T(8,128)(2,1)}), bf16[896,8192]{1,0:T(8,128)(2,1)}) %all-gather.2.cloned.1.call-update) | async-done | bytes 14680080 | tf_op jit(solution)/shard_map/all_gather | solution.py:21
  129.3 15.1 %fusion.11 = f32[2048,2048]{1,0:T(8,128)} fusion(bf16[896,8192]{1,0:T(8,128)(2,1)} %all-gather.2.cloned.1.call-done, s32[]{:T(128)} %select_n.87, s32[]{:T(128)S(6)} %select_n.88), kind=kOutput, calls=%fused_computation.29 | convolution fusion | flops 7516192768 | bytes 24117764 | tf_op jit(solution)/shard_map/dot_general | solution.py:25
  145.1 186.7 %reduce-scatter.2.cloned.1.call-done = f32[1024,2048]{1,0:T(8,128)} async-done(((f32[2048,2048]{1,0:T(8,128)}), f32[1024,2048]{1,0:T(8,128)}) %reduce-scatter.2.cloned.1.call-update) | async-done | bytes 8388624 | tf_op jit(solution)/shard_map/reduce_scatter | solution.py:24
  345.3 153.2 %all-reduce.8.cloned.1.call-done = f32[2048,512]{0,1:T(8,128)} async-done(((f32[2048,512]{0,1:T(8,128)}), f32[2048,512]{0,1:T(8,128)}) %all-reduce.8.cloned.1.call-update) | async-done | bytes 4194320 | tf_op jit(solution)/shard_map/psum | solution.py:12
  501.4 67.2 %all-reduce.14.cloned.1.call-done = (f32[512,1024]{0,1:T(8,128)}, f32[512,512]{0,1:T(8,128)}) async-done(((f32[512,1024]{0,1:T(8,128)}, f32[512,512]{0,1:T(8,128)}), (f32[512,1024]{0,1:T(8,128)}, f32[512,512]{0,1:T(8,128)})) %all-reduce.14.cloned.1.call-update) | async-done | bytes 3145744 | tf_op jit(solution)/shard_map/psum | solution.py:12
  571.7 11.7 cholesky.286
  583.6 9.8 custom-call.31
  594.1 11.7 cholesky.305
  605.8 10.0 custom-call.32
  616.4 11.7 cholesky.326
  628.2 9.8 custom-call.33
  638.6 11.7 cholesky.343
  663.0 39.3 %custom-call.34 = f32[4,128,128]{1,2,0:T(8,128)S(1)} custom-call(f32[4,128,128]{2,1,0:T(8,128)S(1)} %get-tuple-element.38), custom_call_target="InvertDiagBlocksLowerTriangular" | custom-call | tf_op jit(solution)/shard_map/triangular_solve/custom-call.3 | solution.py:66
  727.0 17.2 %convolution_subtract_fusion = f32[2048,1024]{0,1:T(8,128)S(1)} fusion(f32[2048,1024]{0,1:T(8,128)S(1)} %bitcast.135, f32[128,1024]{1,0:T(8,128)} %fusion.106, f32[128,1024]{1,0:T(8,128)} %copy-done.9, f32[128,1024]{1,0:T(8,128)} %copy-done.7, f32[128,1024]{1,0:T(8,128)} %copy-done.4, f32[2048,128]{0,1:T(8,128)} %fusion.107, f32[2048,128]{0,1:T(8,128)} %copy-done.5, ...), kind=kOutput, calls=%fused_computation.28 | convolution fusion | flops 12891717632 | bytes 23068672 | tf_op jit(solution)/shard_map/dot_general | solution.py:70
  753.1 153.3 %all-reduce.10.cloned.1.call-done = f32[2048,512]{0,1:T(8,128)} async-done(((f32[2048,512]{0,1:T(8,128)}), f32[2048,512]{0,1:T(8,128)}) %all-reduce.10.cloned.1.call-update) | async-done | bytes 4194320 | tf_op jit(solution)/shard_map/psum | solution.py:12
  910.5 9.8 gather_fusion.1
  920.3 9.5 copy.4
  933.3 11.6 gather_fusion
  944.9 31.7 %all-reduce.12.cloned.1.call-done = (f32[512,1024]{0,1:T(8,128)}, f32[512,512]{0,1:T(8,128)}) async-done(((f32[512,1024]{0,1:T(8,128)}, f32[512,512]{0,1:T(8,128)}), (f32[512,1024]{0,1:T(8,128)}, f32[512,512]{0,1:T(8,128)})) %all-reduce.12.cloned.1.call-update) | async-done | bytes 3145744 | tf_op jit(solution)/shard_map/psum | solution.py:12
  979.6 11.7 cholesky.358
  991.5 9.8 custom-call.36
  1002.0 11.7 cholesky.377
  1013.7 10.0 custom-call.37
  1024.4 11.7 cholesky.398
  1036.1 9.8 custom-call.38
  1046.5 11.7 cholesky.415
  1072.3 39.3 %custom-call.39 = f32[4,128,128]{1,2,0:T(8,128)S(1)} custom-call(f32[4,128,128]{2,1,0:T(8,128)S(1)} %get-tuple-element.40), custom_call_target="InvertDiagBlocksLowerTriangular" | custom-call | tf_op jit(solution)/shard_map/triangular_solve/custom-call.3 | solution.py:66
  1122.9 9.8 gather_fusion.3
  1132.7 9.6 copy.7
  1158.4 11.2 gather_fusion.2
  1169.6 29.6 %fusion.8 = f32[2048,1024]{0,1:T(8,128)} fusion(f32[2048,1024]{0,1:T(8,128)} %copy.7, f32[1024,2048]{1,0:T(8,128)} %gather_fusion.2, f32[2048,1024]{0,1:T(8,128)} %copy.4, f32[1024,2048]{1,0:T(8,128)} %gather_fusion, f32[2048,1024]{0,1:T(8,128)} %copy-done.1, s32[2048]{0:T(1024)S(1)} %iota_add_fusion, pred[1024]{0:T(1024)(128)(4,1)S(1)} %get-tuple-element.98, ...), kind=kOutput, calls=%fused_computation.20 | convolution fusion | flops 12935757824 | bytes 56647680 | tf_op jit(solution)/shard_map/dot_general | solution.py:70
  1199.2 9.2 copy.9
  (178 shorter events, 132.9 us)
Async XLA Ops:
  6.5 122.7 %all-gather.2.cloned.1.call-start = ((), (), s32[]{:S(2)}) async-start(), calls=%async_computation.1 | async-start | bytes 15597568 | tf_op jit(solution)/shard_map/all_gather | solution.py:21
  7.3 324.5 %reduce-scatter.2.cloned.1.call-start = ((), (), s32[]{:S(2)}) async-start(), calls=%async_computation.2 | async-start | bytes 25165824 | tf_op jit(solution)/shard_map/reduce_scatter | solution.py:24
  144.3 0.8 copy-start.19
  144.3 187.5 %dynamic-slice-start = ((f32[8192]{0:T(1024)}, s32[]{:T(128)}), f32[2048]{0:T(1024)S(1)}, s32[]{:S(2)}) async-start(f32[8192]{0:T(1024)} %param.12, s32[]{:T(128)} %select_n.87), calls=%async_computation.9 | async-start | bytes 16896 | tf_op jit(solution)/shard_map/dynamic_slice | solution.py:37
  144.4 354.1 %all-reduce.8.cloned.1.call-start = ((), (), s32[]{:S(2)}) async-start(), calls=%async_computation.3 | async-start | bytes 8388608 | tf_op jit(solution)/shard_map/psum | solution.py:12
  336.1 3.4 copy-start
  342.0 226.6 %all-reduce.14.cloned.1.call-start = ((), (), s32[]{:S(2)}) async-start(), calls=%async_computation.6 | async-start | bytes 6291456 | tf_op jit(solution)/shard_map/psum | solution.py:12
  500.8 405.6 %all-reduce.10.cloned.1.call-start = ((), (), s32[]{:S(2)}) async-start(), calls=%async_computation.4 | async-start | bytes 8388608 | tf_op jit(solution)/shard_map/psum | solution.py:12
  663.0 51.9 %copy-start.14 = (f32[512,512]{1,0:T(8,128)}, f32[512,512]{1,0:T(8,128)S(1)}, u32[]{:S(2)}) copy-start(f32[512,512]{1,0:T(8,128)S(1)} %get-tuple-element.218) | copy-start | bytes 3145732
  702.3 4.8 copy-start.17
  704.2 8.2 copy-start.4
  706.4 7.4 copy-start.11
  707.1 7.8 copy-start.7
  709.6 6.4 copy-start.9
  716.0 11.0 slice-start
  717.1 9.9 copy-start.2
  720.0 6.9 slice-start.1
  721.1 3.7 copy-start.5
  744.2 3.4 copy-start.1
  749.9 226.7 %all-reduce.12.cloned.1.call-start = ((), (), s32[]{:S(2)}) async-start(), calls=%async_computation.5 | async-start | bytes 6291456 | tf_op jit(solution)/shard_map/psum | solution.py:12
  920.3 9.5 copy-start.3
  920.3 9.5 copy-start.6
  1072.3 49.1 %copy-start.13 = (f32[512,512]{1,0:T(8,128)}, f32[512,512]{1,0:T(8,128)S(1)}, u32[]{:S(2)}) copy-start(f32[512,512]{1,0:T(8,128)S(1)} %get-tuple-element.217) | copy-start | bytes 3145732
  1111.7 4.5 copy-start.16
  1118.7 3.4 copy-start.12
  1122.1 0.8 copy-start.18
  1142.3 5.9 copy-start.10
  1151.5 6.9 copy-start.8
  1155.9 2.5 copy-start.15
Sparse Core Ops, SparseCore 0:
  9.4 119.7 all-gather.1
  144.5 187.2 reduce-scatter.1
  342.1 156.2 all-reduce.7
  501.0 67.6 all-reduce.13
  750.0 156.3 all-reduce.9
  908.9 67.6 all-reduce.11
where the time goes:
time: 1220 us
  waiting for transfers between devices  715 us (59%)
  other arithmetic  268 us (22%)
  matrix products  114 us (9%)
  local copies, waits for them, and re-layouts  98 us (8%)
  between operations  20 us (2%)
    psum x4, waiting for transfers between devices, from_root(): return lax.psum(jnp.where(mine, array, jnp.zeros_like(array)), axis)  405 us
    reduce_scatter x1, waiting for transfers between devices, body(): lax.psum_scatter(lax.dot_general(col_block, row_block, (((0,), (0,)), (()...  187 us
    another operation x29, other arithmetic, body(): factor = jnp.linalg.cholesky(diag_block)  158 us
    all_gather x1, waiting for transfers between devices, body(): lax.all_gather(pair_elements, ('grow', 'gcol'), axis=1, tiled=True)  122 us
    another operation x7, other arithmetic, body(): lax.linalg.triangular_solve(factor, panel_cols, left_side=False, lower=Tr...  85 us
    dot_general x2, matrix products, body(): jnp.dot(low_rows, low_cols, precision=lax.Precision.HIGHEST)  46.8 us
    gather x4, local copies, waits for them, and re-layouts, body(): row_vals = jnp.take(low_cols, jnp.clip(row_pos[:, 0], 0, PANEL - 1), axis=0)  38.7 us
    another operation x14, matrix products, body(): lax.linalg.triangular_solve(factor, panel_cols, left_side=False, lower=Tr...  26.6 us
  transfers between devices with their start and end apart: 6, of which 6 were waited for; matrix products, arithmetic and copies ran while one was open for 3% of the time, Pallas kernels for 0%

commit v1 on v0

--- a/solution.py
+++ b/solution.py
@@ -18,7 +18,29 @@
     tile_cols = grid_total // (lax.axis_size("gcol") * lax.axis_size("pair"))
     row_index = lax.axis_index("grow")
     col_index = lax.axis_index("gcol")
-    gathered = lax.all_gather(pair_elements, ("grow", "gcol"), axis=1, tiled=True)
+    peers, place, rows = (
+        lax.axis_size(("grow", "gcol")),
+        lax.axis_index(("grow", "gcol")),
+        pair_elements.shape[1],
+    )
+    ahead = [(i, (i + 1) % peers) for i in range(peers)]
+    left = [(i, (i - 1) % peers) for i in range(peers)]
+    gathered = jnp.zeros(
+        (*pair_elements.shape[:1], peers * rows, *pair_elements.shape[1 + 1 :]), pair_elements.dtype
+    )
+    gathered = lax.dynamic_update_slice_in_dim(gathered, pair_elements, place * rows, axis=1)
+    from_left = from_right = pair_elements
+    halfway = peers // 2
+    for step in range(1, halfway + 1):
+        from_left = lax.ppermute(from_left, ("grow", "gcol"), ahead)
+        gathered = lax.dynamic_update_slice_in_dim(
+            gathered, from_left, (place - step) % peers * rows, axis=1
+        )
+        if step < peers - halfway:
+            from_right = lax.ppermute(from_right, ("grow", "gcol"), left)
+            gathered = lax.dynamic_update_slice_in_dim(
+                gathered, from_right, (place + step) % peers * rows, axis=1
+            )
     row_block = lax.dynamic_slice_in_dim(gathered, row_index * tile_rows, tile_rows, 1)
     col_block = lax.dynamic_slice_in_dim(gathered, col_index * tile_rows, tile_rows, 1)
     flipped = lax.psum_scatter(

time: 1220 us -> 1410 us (1.16)
  waiting for transfers between devices: 715 us -> 841 us
  local copies, waits for them, and re-layouts: 98 us -> 129 us
  starting transfers between devices: 0.73 us -> 25.2 us
    ppermute x0 -> x15, waiting for transfers between devices: none -> 244 us  [the longest x7 139 us: body(): from_right = lax.ppermute(from_right, ('grow', 'gcol'), left)]
    all_gather x1 -> x0, waiting for transfers between devices: 122 us -> none  [body(): lax.all_gather(pair_elements, ('grow', 'gcol'), axis=1, tiled=True)]
    ppermute x0 -> x15, starting transfers between devices: none -> 24.9 us  [the longest x8 18.1 us: body(): from_left = lax.ppermute(from_left, ('grow', 'gcol'), ahead)]
    dynamic_update_slice x0 -> x16, local copies, waits for them, and re-layouts: none -> 22.4 us  [the longest x7 10.8 us: body(): lax.dynamic_update_slice_in_dim(gathered, from_right, (place + step) % pe...]
  transfers between devices with their start and end apart: 6 -> 20, of which waited for: 6 -> 20; matrix products, arithmetic and copies ran while one was open for 3% -> 5% of each run, Pallas kernels for 0% -> 0%
where the time goes in v1:
time: 1410 us; the launch traced here: 1400 us
  waiting for transfers between devices  841 us (60%)
  other arithmetic  269 us (19%)
  local copies, waits for them, and re-layouts  129 us (9%)
  matrix products  114 us (8%)
  starting transfers between devices  25.2 us (2%)
  between operations  19.3 us (1%)
    psum x4, waiting for transfers between devices, from_root(): return lax.psum(jnp.where(mine, array, jnp.zeros_like(array)), axis)  406 us
    reduce_scatter x1, waiting for transfers between devices, body(): lax.psum_scatter(lax.dot_general(col_block, row_block, (((0,), (0,)), (()...  190 us
    another operation x29, other arithmetic, body(): factor = jnp.linalg.cholesky(diag_block)  158 us
    ppermute x7, waiting for transfers between devices, body(): from_right = lax.ppermute(from_right, ('grow', 'gcol'), left)  139 us
    ppermute x8, waiting for transfers between devices, body(): from_left = lax.ppermute(from_left, ('grow', 'gcol'), ahead)  105 us
    another operation x7, other arithmetic, body(): lax.linalg.triangular_solve(factor, panel_cols, left_side=False, lower=Tr...  85.4 us
    dot_general x2, matrix products, body(): jnp.dot(low_rows, low_cols, precision=lax.Precision.HIGHEST)  46.9 us
    gather x4, local copies, waits for them, and re-layouts, body(): row_vals = jnp.take(low_cols, jnp.clip(row_pos[:, 0], 0, PANEL - 1), axis=0)  38.4 us
  transfers between devices with their start and end apart: 20, of which 20 were waited for; matrix products, arithmetic and copies ran while one was open for 5% of the time, Pallas kernels for 0%

profile of v1, /device:TPU:0, one launch (start us, length us, event | category | flops | bytes accessed | tf_op | source)
XLA Modules:
  0.0 1396.7 jit_solution(17436879968313937015)
XLA Ops:
  12.0 20.4 %collective-permute-done = bf16[896,512]{1,0:T(8,128)(2,1)S(1)} collective-permute-done((bf16[896,512]{1,0:T(8,128)(2,1)}, bf16[896,512]{1,0:T(8,128)(2,1)S(1)}, u32[]{:S(2)}, u32[]{:S(2)}) %collective-permute-start) | collective-permute-done | bytes 917536 | tf_op jit(solution)/shard_map/ppermute | solution.py:35
  33.0 18.2 %collective-permute-done.1 = bf16[896,512]{1,0:T(8,128)(2,1)S(1)} collective-permute-done((bf16[896,512]{1,0:T(8,128)(2,1)}, bf16[896,512]{1,0:T(8,128)(2,1)S(1)}, u32[]{:S(2)}, u32[]{:S(2)}) %collective-permute-start.1) | collective-permute-done | bytes 917536 | tf_op jit(solution)/shard_map/ppermute | solution.py:40
  54.8 15.4 %collective-permute-done.2 = bf16[896,512]{1,0:T(8,128)(2,1)S(1)} collective-permute-done((bf16[896,512]{1,0:T(8,128)(2,1)S(1)}, bf16[896,512]{1,0:T(8,128)(2,1)S(1)}, u32[]{:S(2)}, u32[]{:S(2)}) %collective-permute-start.2) | collective-permute-done | bytes 917536 | tf_op jit(solution)/shard_map/ppermute | solution.py:35
  72.4 21.1 %collective-permute-done.3 = bf16[896,512]{1,0:T(8,128)(2,1)S(1)} collective-permute-done((bf16[896,512]{1,0:T(8,128)(2,1)S(1)}, bf16[896,512]{1,0:T(8,128)(2,1)S(1)}, u32[]{:S(2)}, u32[]{:S(2)}) %collective-permute-start.3) | collective-permute-done | bytes 917536 | tf_op jit(solution)/shard_map/ppermute | solution.py:40
  94.2 15.0 %collective-permute-done.4 = bf16[896,512]{1,0:T(8,128)(2,1)S(1)} collective-permute-done((bf16[896,512]{1,0:T(8,128)(2,1)S(1)}, bf16[896,512]{1,0:T(8,128)(2,1)S(1)}, u32[]{:S(2)}, u32[]{:S(2)}) %collective-permute-start.4) | collective-permute-done | bytes 917536 | tf_op jit(solution)/shard_map/ppermute | solution.py:35
  111.8 22.1 %collective-permute-done.5 = bf16[896,512]{1,0:T(8,128)(2,1)S(1)} collective-permute-done((bf16[896,512]{1,0:T(8,128)(2,1)S(1)}, bf16[896,512]{1,0:T(8,128)(2,1)S(1)}, u32[]{:S(2)}, u32[]{:S(2)}) %collective-permute-start.5) | collective-permute-done | bytes 917536 | tf_op jit(solution)/shard_map/ppermute | solution.py:40
  133.9 14.7 %collective-permute-done.6 = bf16[896,512]{1,0:T(8,128)(2,1)S(1)} collective-permute-done((bf16[896,512]{1,0:T(8,128)(2,1)S(1)}, bf16[896,512]{1,0:T(8,128)(2,1)S(1)}, u32[]{:S(2)}, u32[]{:S(2)}) %collective-permute-start.6) | collective-permute-done | bytes 917536 | tf_op jit(solution)/shard_map/ppermute | solution.py:35
  152.1 22.2 %collective-permute-done.7 = bf16[896,512]{1,0:T(8,128)(2,1)} collective-permute-done((bf16[896,512]{1,0:T(8,128)(2,1)S(1)}, bf16[896,512]{1,0:T(8,128)(2,1)}, u32[]{:S(2)}, u32[]{:S(2)}) %collective-permute-start.7) | collective-permute-done | bytes 917536 | tf_op jit(solution)/shard_map/ppermute | solution.py:40
  174.3 13.7 collective-permute-done.8
  190.6 23.8 %collective-permute-done.9 = bf16[896,512]{1,0:T(8,128)(2,1)} collective-permute-done((bf16[896,512]{1,0:T(8,128)(2,1)}, bf16[896,512]{1,0:T(8,128)(2,1)}, u32[]{:S(2)}, u32[]{:S(2)}) %collective-permute-start.9) | collective-permute-done | bytes 917536 | tf_op jit(solution)/shard_map/ppermute | solution.py:40
  236.0 18.4 %collective-permute-done.11 = bf16[896,512]{1,0:T(8,128)(2,1)} collective-permute-done((bf16[896,512]{1,0:T(8,128)(2,1)}, bf16[896,512]{1,0:T(8,128)(2,1)}, u32[]{:S(2)}, u32[]{:S(2)}) %collective-permute-start.11) | collective-permute-done | bytes 917536 | tf_op jit(solution)/shard_map/ppermute | solution.py:40
  255.5 11.4 collective-permute-done.12
  281.5 12.8 collective-permute-done.13
  306.0 14.9 %fusion.11 = f32[2048,2048]{1,0:T(8,128)} fusion(bf16[896,8192]{1,0:T(8,128)(2,1)} %constant_dynamic-update-slice_fusion.2, s32[]{:T(128)} %select_n.198, s32[]{:T(128)S(6)} %select_n.230), kind=kOutput, calls=%fused_computation.29 | convolution fusion | flops 7516192768 | bytes 24117764 | tf_op jit(solution)/shard_map/dot_general | solution.py:47
  321.7 190.4 %reduce-scatter.2.cloned.1.call-done = f32[1024,2048]{1,0:T(8,128)} async-done(((f32[2048,2048]{1,0:T(8,128)}), f32[1024,2048]{1,0:T(8,128)}) %reduce-scatter.2.cloned.1.call-update) | async-done | bytes 8388624 | tf_op jit(solution)/shard_map/reduce_scatter | solution.py:46
  525.6 153.2 %all-reduce.8.cloned.1.call-done = f32[2048,512]{0,1:T(8,128)} async-done(((f32[2048,512]{0,1:T(8,128)}), f32[2048,512]{0,1:T(8,128)}) %all-reduce.8.cloned.1.call-update) | async-done | bytes 4194320 | tf_op jit(solution)/shard_map/psum | solution.py:12
  681.4 67.7 %all-reduce.14.cloned.1.call-done = (f32[512,1024]{0,1:T(8,128)}, f32[512,512]{0,1:T(8,128)}) async-done(((f32[512,1024]{0,1:T(8,128)}, f32[512,512]{0,1:T(8,128)}), (f32[512,1024]{0,1:T(8,128)}, f32[512,512]{0,1:T(8,128)})) %all-reduce.14.cloned.1.call-update) | async-done | bytes 3145744 | tf_op jit(solution)/shard_map/psum | solution.py:12
  752.1 11.7 cholesky.286
  774.5 11.7 cholesky.305
  797.1 11.7 cholesky.326
  819.3 11.7 cholesky.343
  843.9 39.3 %custom-call.34 = f32[4,128,128]{1,2,0:T(8,128)S(1)} custom-call(f32[4,128,128]{2,1,0:T(8,128)S(1)} %get-tuple-element.38), custom_call_target="InvertDiagBlocksLowerTriangular" | custom-call | tf_op jit(solution)/shard_map/triangular_solve/custom-call.3 | solution.py:88
  908.1 17.2 %convolution_subtract_fusion = f32[2048,1024]{0,1:T(8,128)S(1)} fusion(f32[2048,1024]{0,1:T(8,128)S(1)} %bitcast.135, f32[128,1024]{1,0:T(8,128)} %fusion.106, f32[128,1024]{1,0:T(8,128)} %copy-done.9, f32[128,1024]{1,0:T(8,128)} %copy-done.7, f32[128,1024]{1,0:T(8,128)} %copy-done.4, f32[2048,128]{0,1:T(8,128)} %fusion.107, f32[2048,128]{0,1:T(8,128)} %copy-done.5, ...), kind=kOutput, calls=%fused_computation.28 | convolution fusion | flops 12891717632 | bytes 23068672 | tf_op jit(solution)/shard_map/dot_general | solution.py:92
  934.3 153.3 %all-reduce.10.cloned.1.call-done = f32[2048,512]{0,1:T(8,128)} async-done(((f32[2048,512]{0,1:T(8,128)}), f32[2048,512]{0,1:T(8,128)}) %all-reduce.10.cloned.1.call-update) | async-done | bytes 4194320 | tf_op jit(solution)/shard_map/psum | solution.py:12
  1114.4 11.3 gather_fusion
  1125.7 32.0 %all-reduce.12.cloned.1.call-done = (f32[512,1024]{0,1:T(8,128)}, f32[512,512]{0,1:T(8,128)}) async-done(((f32[512,1024]{0,1:T(8,128)}, f32[512,512]{0,1:T(8,128)}), (f32[512,1024]{0,1:T(8,128)}, f32[512,512]{0,1:T(8,128)})) %all-reduce.12.cloned.1.call-update) | async-done | bytes 3145744 | tf_op jit(solution)/shard_map/psum | solution.py:12
  1160.7 11.7 cholesky.358
  1183.1 11.7 cholesky.377
  1205.5 11.7 cholesky.398
  1227.7 11.7 cholesky.415
  1254.0 39.3 %custom-call.39 = f32[4,128,128]{1,2,0:T(8,128)S(1)} custom-call(f32[4,128,128]{2,1,0:T(8,128)S(1)} %get-tuple-element.40), custom_call_target="InvertDiagBlocksLowerTriangular" | custom-call | tf_op jit(solution)/shard_map/triangular_solve/custom-call.3 | solution.py:88
  1351.1 29.7 %fusion.8 = f32[2048,1024]{0,1:T(8,128)} fusion(f32[2048,1024]{0,1:T(8,128)} %copy.7, f32[1024,2048]{1,0:T(8,128)} %gather_fusion.2, f32[2048,1024]{0,1:T(8,128)} %copy.4, f32[1024,2048]{1,0:T(8,128)} %gather_fusion, f32[2048,1024]{0,1:T(8,128)} %copy-done.1, s32[2048]{0:T(1024)S(1)} %iota_add_fusion, pred[1024]{0:T(1024)(128)(4,1)S(1)} %get-tuple-element.98, ...), kind=kOutput, calls=%fused_computation.20 | convolution fusion | flops 12935757824 | bytes 56647680 | tf_op jit(solution)/shard_map/dot_general | solution.py:92
  (244 shorter events, 322.4 us)
Async XLA Ops:
  6.5 505.5 %reduce-scatter.2.cloned.1.call-start = ((), (), s32[]{:S(2)}) async-start(), calls=%async_computation.1 | async-start | bytes 25165824 | tf_op jit(solution)/shard_map/reduce_scatter | solution.py:46
  6.5 25.9 %collective-permute-start = (bf16[896,512]{1,0:T(8,128)(2,1)}, bf16[896,512]{1,0:T(8,128)(2,1)S(1)}, u32[]{:S(2)}, u32[]{:S(2)}) collective-permute-start(bf16[896,512]{1,0:T(8,128)(2,1)} %param.11), channel_id=1, source_target_pairs={{0,1},{1,2},{2,3},{3,4},{4,5},{5,6},{6,7},{7,8},{8,9},{9,10},{10,1... | collective-permute-start | bytes 2752520 | tf_op jit(solution)/shard_map/ppermute | solution.py:35
  9.6 41.7 %collective-permute-start.1 = (bf16[896,512]{1,0:T(8,128)(2,1)}, bf16[896,512]{1,0:T(8,128)(2,1)S(1)}, u32[]{:S(2)}, u32[]{:S(2)}) collective-permute-start(bf16[896,512]{1,0:T(8,128)(2,1)} %param.11), channel_id=1, source_target_pairs={{0,15},{1,0},{2,1},{3,2},{4,3},{5,4},{6,5},{7,6},{8,7},{9,8},{10,9... | collective-permute-start | bytes 2752520 | tf_op jit(solution)/shard_map/ppermute | solution.py:40
  32.4 37.9 %collective-permute-start.2 = (bf16[896,512]{1,0:T(8,128)(2,1)S(1)}, bf16[896,512]{1,0:T(8,128)(2,1)S(1)}, u32[]{:S(2)}, u32[]{:S(2)}) collective-permute-start(bf16[896,512]{1,0:T(8,128)(2,1)S(1)} %collective-permute-done), channel_id=1, source_target_pairs={{0,1},{1,2},{2,3},{3,4},{4,5},{5,6},{6,7},{7,8},{8,9},{9,10},{10,1... | collective-permute-start | bytes 2752520 | tf_op jit(solution)/shard_map/ppermute | solution.py:35
  51.2 42.2 %collective-permute-start.3 = (bf16[896,512]{1,0:T(8,128)(2,1)S(1)}, bf16[896,512]{1,0:T(8,128)(2,1)S(1)}, u32[]{:S(2)}, u32[]{:S(2)}) collective-permute-start(bf16[896,512]{1,0:T(8,128)(2,1)S(1)} %collective-permute-done.1), channel_id=1, source_target_pairs={{0,15},{1,0},{2,1},{3,2},{4,3},{5,4},{6,5},{7,6},{8,7},{9,8},{10,9... | collective-permute-start | bytes 2752520 | tf_op jit(solution)/shard_map/ppermute | solution.py:40
  70.3 23.2 %copy-start.20 = (bf16[896,512]{1,0:T(8,128)(2,1)}, bf16[896,512]{1,0:T(8,128)(2,1)S(1)}, u32[]{:S(2)}) copy-start(bf16[896,512]{1,0:T(8,128)(2,1)S(1)} %collective-permute-done.2) | copy-start | bytes 2752516
  70.3 39.0 %collective-permute-start.4 = (bf16[896,512]{1,0:T(8,128)(2,1)S(1)}, bf16[896,512]{1,0:T(8,128)(2,1)S(1)}, u32[]{:S(2)}, u32[]{:S(2)}) collective-permute-start(bf16[896,512]{1,0:T(8,128)(2,1)S(1)} %collective-permute-done.2), channel_id=1, source_target_pairs={{0,1},{1,2},{2,3},{3,4},{4,5},{5,6},{6,7},{7,8},{8,9},{9,10},{10,1... | collective-permute-start | bytes 2752520 | tf_op jit(solution)/shard_map/ppermute | solution.py:35
  93.5 15.8 %copy-start.22 = (bf16[896,512]{1,0:T(8,128)(2,1)}, bf16[896,512]{1,0:T(8,128)(2,1)S(1)}, u32[]{:S(2)}) copy-start(bf16[896,512]{1,0:T(8,128)(2,1)S(1)} %collective-permute-done.3) | copy-start | bytes 2752516
  93.5 40.4 %collective-permute-start.5 = (bf16[896,512]{1,0:T(8,128)(2,1)S(1)}, bf16[896,512]{1,0:T(8,128)(2,1)S(1)}, u32[]{:S(2)}, u32[]{:S(2)}) collective-permute-start(bf16[896,512]{1,0:T(8,128)(2,1)S(1)} %collective-permute-done.3), channel_id=1, source_target_pairs={{0,15},{1,0},{2,1},{3,2},{4,3},{5,4},{6,5},{7,6},{8,7},{9,8},{10,9... | collective-permute-start | bytes 2752520 | tf_op jit(solution)/shard_map/ppermute | solution.py:40
  109.3 78.7 %copy-start.26 = (bf16[896,512]{1,0:T(8,128)(2,1)}, bf16[896,512]{1,0:T(8,128)(2,1)S(1)}, u32[]{:S(2)}) copy-start(bf16[896,512]{1,0:T(8,128)(2,1)S(1)} %collective-permute-done.4) | copy-start | bytes 2752516
  109.3 39.4 %collective-permute-start.6 = (bf16[896,512]{1,0:T(8,128)(2,1)S(1)}, bf16[896,512]{1,0:T(8,128)(2,1)S(1)}, u32[]{:S(2)}, u32[]{:S(2)}) collective-permute-start(bf16[896,512]{1,0:T(8,128)(2,1)S(1)} %collective-permute-done.4), channel_id=1, source_target_pairs={{0,1},{1,2},{2,3},{3,4},{4,5},{5,6},{6,7},{7,8},{8,9},{9,10},{10,1... | collective-permute-start | bytes 2752520 | tf_op jit(solution)/shard_map/ppermute | solution.py:35
  133.9 56.7 %copy-start.28 = (bf16[896,512]{1,0:T(8,128)(2,1)}, bf16[896,512]{1,0:T(8,128)(2,1)S(1)}, u32[]{:S(2)}) copy-start(bf16[896,512]{1,0:T(8,128)(2,1)S(1)} %collective-permute-done.5) | copy-start | bytes 2752516
  133.9 40.4 %collective-permute-start.7 = (bf16[896,512]{1,0:T(8,128)(2,1)S(1)}, bf16[896,512]{1,0:T(8,128)(2,1)}, u32[]{:S(2)}, u32[]{:S(2)}) collective-permute-start(bf16[896,512]{1,0:T(8,128)(2,1)S(1)} %collective-permute-done.5), channel_id=1, source_target_pairs={{0,15},{1,0},{2,1},{3,2},{4,3},{5,4},{6,5},{7,6},{8,7},{9,8},{10,9... | collective-permute-start | bytes 2752520 | tf_op jit(solution)/shard_map/ppermute | solution.py:40
  149.6 38.4 %collective-permute-start.8 = (bf16[896,512]{1,0:T(8,128)(2,1)S(1)}, bf16[896,512]{1,0:T(8,128)(2,1)}, u32[]{:S(2)}, u32[]{:S(2)}) collective-permute-start(bf16[896,512]{1,0:T(8,128)(2,1)S(1)} %collective-permute-done.6), channel_id=1, source_target_pairs={{0,1},{1,2},{2,3},{3,4},{4,5},{5,6},{6,7},{7,8},{8,9},{9,10},{10,1... | collective-permute-start | bytes 2752520 | tf_op jit(solution)/shard_map/ppermute | solution.py:35
  174.3 40.1 %collective-permute-start.9 = (bf16[896,512]{1,0:T(8,128)(2,1)}, bf16[896,512]{1,0:T(8,128)(2,1)}, u32[]{:S(2)}, u32[]{:S(2)}) collective-permute-start(bf16[896,512]{1,0:T(8,128)(2,1)} %collective-permute-done.7), channel_id=1, source_target_pairs={{0,15},{1,0},{2,1},{3,2},{4,3},{5,4},{6,5},{7,6},{8,7},{9,8},{10,9... | collective-permute-start | bytes 2752520 | tf_op jit(solution)/shard_map/ppermute | solution.py:40
  188.0 39.5 %collective-permute-start.10 = (bf16[896,512]{1,0:T(8,128)(2,1)}, bf16[896,512]{1,0:T(8,128)(2,1)}, u32[]{:S(2)}, u32[]{:S(2)}) collective-permute-start(bf16[896,512]{1,0:T(8,128)(2,1)} %collective-permute-done.8), channel_id=1, source_target_pairs={{0,1},{1,2},{2,3},{3,4},{4,5},{5,6},{6,7},{7,8},{8,9},{9,10},{10,1... | collective-permute-start | bytes 2752520 | tf_op jit(solution)/shard_map/ppermute | solution.py:35
  190.6 30.9 %copy-start.19 = (bf16[896,512]{1,0:T(8,128)(2,1)S(1)}, bf16[896,512]{1,0:T(8,128)(2,1)}, u32[]{:S(2)}) copy-start(bf16[896,512]{1,0:T(8,128)(2,1)} %param.11) | copy-start | bytes 2752516
  214.4 40.0 %collective-permute-start.11 = (bf16[896,512]{1,0:T(8,128)(2,1)}, bf16[896,512]{1,0:T(8,128)(2,1)}, u32[]{:S(2)}, u32[]{:S(2)}) collective-permute-start(bf16[896,512]{1,0:T(8,128)(2,1)} %collective-permute-done.9), channel_id=1, source_target_pairs={{0,15},{1,0},{2,1},{3,2},{4,3},{5,4},{6,5},{7,6},{8,7},{9,8},{10,9... | collective-permute-start | bytes 2752520 | tf_op jit(solution)/shard_map/ppermute | solution.py:40
  221.5 11.5 copy-start.23
  221.5 12.6 copy-start.27
  222.5 12.5 copy-start.29
  227.5 39.4 %collective-permute-start.12 = (bf16[896,512]{1,0:T(8,128)(2,1)}, bf16[896,512]{1,0:T(8,128)(2,1)S(1)}, u32[]{:S(2)}, u32[]{:S(2)}) collective-permute-start(bf16[896,512]{1,0:T(8,128)(2,1)} %collective-permute-done.10), channel_id=1, source_target_pairs={{0,1},{1,2},{2,3},{3,4},{4,5},{5,6},{6,7},{7,8},{8,9},{9,10},{10,1... | collective-permute-start | bytes 2752520 | tf_op jit(solution)/shard_map/ppermute | solution.py:35
  231.0 23.5 %copy-start.25 = (bf16[896,512]{1,0:T(8,128)(2,1)S(1)}, bf16[896,512]{1,0:T(8,128)(2,1)}, u32[]{:S(2)}) copy-start(bf16[896,512]{1,0:T(8,128)(2,1)} %copy-done.24) | copy-start | bytes 2752516
  254.5 39.8 %collective-permute-start.13 = (bf16[896,512]{1,0:T(8,128)(2,1)}, bf16[896,512]{1,0:T(8,128)(2,1)S(1)}, u32[]{:S(2)}, u32[]{:S(2)}) collective-permute-start(bf16[896,512]{1,0:T(8,128)(2,1)} %collective-permute-done.11), channel_id=1, source_target_pairs={{0,15},{1,0},{2,1},{3,2},{4,3},{5,4},{6,5},{7,6},{8,7},{9,8},{10,9... | collective-permute-start | bytes 2752520 | tf_op jit(solution)/shard_map/ppermute | solution.py:40
  266.8 38.1 %collective-permute-start.14 = (bf16[896,512]{1,0:T(8,128)(2,1)S(1)}, bf16[896,512]{1,0:T(8,128)(2,1)S(1)}, u32[]{:S(2)}, u32[]{:S(2)}) collective-permute-start(bf16[896,512]{1,0:T(8,128)(2,1)S(1)} %collective-permute-done.12), channel_id=1, source_target_pairs={{0,1},{1,2},{2,3},{3,4},{4,5},{5,6},{6,7},{7,8},{8,9},{9,10},{10,1... | collective-permute-start | bytes 2752520 | tf_op jit(solution)/shard_map/ppermute | solution.py:35
  320.9 191.1 %dynamic-slice-start = ((f32[8192]{0:T(1024)}, s32[]{:T(128)}), f32[2048]{0:T(1024)S(1)}, s32[]{:S(2)}) async-start(f32[8192]{0:T(1024)} %param.12, s32[]{:T(128)} %select_n.198), calls=%async_computation.8 | async-start | bytes 16896 | tf_op jit(solution)/shard_map/dynamic_slice | solution.py:59
  321.0 357.8 %all-reduce.8.cloned.1.call-start = ((), (), s32[]{:S(2)}) async-start(), calls=%async_computation.2 | async-start | bytes 8388608 | tf_op jit(solution)/shard_map/psum | solution.py:12
  522.3 226.8 %all-reduce.14.cloned.1.call-start = ((), (), s32[]{:S(2)}) async-start(), calls=%async_computation.5 | async-start | bytes 6291456 | tf_op jit(solution)/shard_map/psum | solution.py:12
  681.2 406.3 %all-reduce.10.cloned.1.call-start = ((), (), s32[]{:S(2)}) async-start(), calls=%async_computation.3 | async-start | bytes 8388608 | tf_op jit(solution)/shard_map/psum | solution.py:12
  843.9 51.9 %copy-start.14 = (f32[512,512]{1,0:T(8,128)}, f32[512,512]{1,0:T(8,128)S(1)}, u32[]{:S(2)}) copy-start(f32[512,512]{1,0:T(8,128)S(1)} %get-tuple-element.217) | copy-start | bytes 3145732
  931.0 226.7 %all-reduce.12.cloned.1.call-start = ((), (), s32[]{:S(2)}) async-start(), calls=%async_computation.4 | async-start | bytes 6291456 | tf_op jit(solution)/shard_map/psum | solution.py:12
  1254.0 49.1 %copy-start.13 = (f32[512,512]{1,0:T(8,128)}, f32[512,512]{1,0:T(8,128)S(1)}, u32[]{:S(2)}) copy-start(f32[512,512]{1,0:T(8,128)S(1)} %get-tuple-element.216) | copy-start | bytes 3145732
  (22 other events, 128.3 us)
Sparse Core Ops, SparseCore 0:
  321.1 190.9 reduce-scatter.1
  522.5 156.2 all-reduce.7
  681.4 67.6 all-reduce.13
  931.1 156.3 all-reduce.9
  1090.0 67.6 all-reduce.11
